TPU v7x, 256 devices: a whole 4x4x8 slice. The times are simulated.
256 devices in a mesh: rows: 4 (over y), cols: 64 (over x, z, core).
Axes of the slice: x: 4, y: 4, z: 8, core: 2. Of those that a mesh axis runs over, the one named last changes fastest.
Arguments:
- sensitivity: bfloat16 [4, 256, 512, 512], P('rows', 'cols'), may hold values from -0.25 to 0.25
- tile_rows: int32 [4, 256], P('rows', 'cols'), may hold values from 0 to 127, as said below
- tile_cols: int32 [4, 256], P('rows', 'cols'), may hold values from 0 to 1, as said below
- kept_counts: int32 [4, 256], P('rows', 'cols'), may hold values from 0 to 512, as said below
- misfit: float32 [262144], P('rows'), may hold values from -6 to 6
- data_weight: float32 [262144], P('rows'), may hold values from 0.3 to 3
- depth_weight: float32 [65536], P('cols'), may hold values from 0.25 to 3
- density: float32 [65536], P('cols'), may hold values from -6 to 6
Outputs:
- new_density: float32 [65536], P('cols')
- new_misfit: float32 [262144], P(('rows', 'cols'))
Inputs may be any that keep to these rules, and one draw needn't show every extreme that they name: Within the 4 slots of one device the pairs (tile_rows, tile_cols) are distinct. Within the 4 slots of one device the pairs (tile_rows, tile_cols) are distinct. A slot with kept_counts 0 is empty, and empty slots come after all live slots of a device; a live slot keeps 512 // 2 or more coefficients; every device has a live slot, and some device has all 4 slots live.
All inputs are finite; a program needn't handle non-finite values.
Results may differ from a plain program's by a relative error of at most 0.033.
Values may be sent and summed in bfloat16 or wider, within the bound.
No kernel may reach another device: no remote copies, remote signals or barrier semaphores. Data moves between devices by JAX's collectives and lax.ppermute only.
A program may use at most 64 MiB of HBM per device.

v0:
```python
import math
import jax
import jax.numpy as jnp
from jax import lax
from jax.sharding import PartitionSpec as P

ITERS = 4
damping = 1.0


def haar_matrix(tile_size):
    rows_index = jnp.arange(tile_size, dtype=jnp.int32)[:, None]
    column_index = jnp.arange(tile_size, dtype=jnp.int32)[None, :]
    levels = jnp.zeros_like(rows_index)
    for bit_shift in range(1, tile_size.bit_length()):
        levels = levels + (rows_index >= 1 << bit_shift).astype(jnp.int32)
    support = jnp.right_shift(tile_size, levels)
    offset = (rows_index - jnp.left_shift(1, levels)) * support
    inside = (column_index >= offset) & (column_index < offset + support)
    polarity = jnp.where(column_index < offset + support // 2, 1.0, -1.0)
    detail = jnp.where(inside, polarity, 0.0) / jnp.sqrt(support.astype(jnp.float32))
    coarse = jnp.full((1, tile_size), 1.0 / math.sqrt(tile_size), jnp.float32)
    return jnp.concatenate([coarse, detail[1:]], axis=0)


def squared_norm(values):
    return lax.psum(jnp.sum(values * values), "cols")


def per_device(
    sensitivity, tile_rows, tile_cols, kept_counts, misfit, data_weight, depth_weight, density
):
    tile_stack = sensitivity[0]
    slot_rows = tile_rows[0]
    slot_cols = tile_cols[0]
    slot_kept = kept_counts[0]
    tile_size = tile_stack.shape[-1]
    data_blocks = misfit.shape[0] // tile_size
    model_blocks = density.shape[0] // tile_size
    wavelet = haar_matrix(tile_size)
    coefficient_index = jnp.arange(tile_size, dtype=jnp.int32)
    live_mask = coefficient_index[None, :] < slot_kept[:, None]
    pick_rows = slot_rows[:, None] == jnp.arange(data_blocks, dtype=jnp.int32)[None, :]
    pick_cols = slot_cols[:, None] == jnp.arange(model_blocks, dtype=jnp.int32)[None, :]
    share_len = misfit.shape[0] // lax.axis_size("cols")
    share_start = lax.axis_index("cols") * share_len
    squared = data_weight * data_weight

    def adjoint_part(weighted):
        data_rows = weighted.reshape(data_blocks, tile_size)
        picked = jnp.dot(
            pick_rows.astype(jnp.bfloat16), data_rows, preferred_element_type=jnp.float32
        ).astype(jnp.bfloat16)
        products = jnp.einsum("sab,sa->sb", tile_stack, picked, preferred_element_type=jnp.float32)
        products = jnp.where(live_mask, products, 0.0)
        block_sums = jnp.dot(
            pick_cols.T.astype(jnp.float32), products, precision=lax.Precision.HIGHEST
        )
        cell_part = jnp.dot(block_sums, wavelet, precision=lax.Precision.HIGHEST).reshape(-1)
        return lax.psum(cell_part, "rows")

    rhs = depth_weight * adjoint_part((squared * misfit).astype(jnp.bfloat16)) - damping * density
    solution = jnp.zeros_like(density)
    residual = rhs
    direction = rhs
    norm_now = squared_norm(residual)
    change = jnp.zeros_like(misfit)
    for iteration in range(ITERS):
        coeffs = jnp.dot(
            (depth_weight * direction).reshape(model_blocks, tile_size),
            wavelet.T,
            precision=lax.Precision.HIGHEST,
        )
        forward_picked = jnp.dot(
            pick_cols.astype(jnp.float32), coeffs, precision=lax.Precision.HIGHEST
        )
        forward_picked = jnp.where(live_mask, forward_picked, 0.0).astype(jnp.bfloat16)
        forward_products = jnp.einsum(
            "sab,sb->sa", tile_stack, forward_picked, preferred_element_type=jnp.float32
        )
        summed = jnp.dot(
            pick_rows.T.astype(jnp.float32), forward_products, precision=lax.Precision.HIGHEST
        )
        partial_data = summed.reshape(-1)
        image_data = lax.psum(partial_data, "cols")
        weighted = (squared * image_data).astype(jnp.bfloat16)
        image_cells = depth_weight * adjoint_part(weighted) + damping * direction
        curvature_sum = lax.psum(jnp.sum(direction * image_cells), "cols")
        step_length = norm_now / curvature_sum
        solution = solution + step_length * direction
        residual = residual - step_length * image_cells
        change = change + step_length * image_data
        if iteration + 1 < ITERS:
            norm_next = squared_norm(residual)
            direction = residual + norm_next / norm_now * direction
            norm_now = norm_next
    new_density = density + depth_weight * solution
    new_misfit = lax.dynamic_slice_in_dim(misfit - change, share_start, share_len)
    return (new_density, new_misfit)


def solution(mesh):
    return jax.shard_map(
        per_device,
        mesh=mesh,
        in_specs=(
            P("rows", "cols", None, None),
            P("rows", "cols"),
            P("rows", "cols"),
            P("rows", "cols"),
            P("rows"),
            P("rows"),
            P("cols"),
            P("cols"),
        ),
        out_specs=(P("cols"), P(("rows", "cols"))),
        check_vma=False,
    )
```

profile of v0, /device:TPU:1, one launch (start us, length us, event | category | flops | bytes accessed | tf_op | source)
XLA Modules:
  0.0 1661.8 jit_solution(10881890196141592567)
XLA Ops:
  7.3 1.2 multiply_convert_fusion.4
  8.9 0.8 fusion.22
  10.8 0.7 convolution_bitcast_fusion.8
  11.4 9.5 psum.119
  21.0 0.9 fusion.42
  23.2 0.8 copy.29
  24.1 178.2 %all-reduce.7.cloned.1.call-done = f32[65536]{0:T(1024)} async-done(((f32[65536]{0:T(1024)}), f32[65536]{0:T(1024)}) %all-reduce.7.cloned.1.call-update) | async-done | bytes 262160 | tf_op jit(solution)/shard_map/psum | solution.py:85
  202.3 1.0 multiply_convert_fusion.3
  203.3 0.7 reshape.190
  204.0 1.1 fusion.23
  205.5 0.9 fusion.51
  206.4 0.7 convolution_bitcast_fusion.7
  207.1 8.4 psum.122
  216.2 125.2 %all-reduce.1 = (f32[]{:T(128)}, f32[]{:T(128)}) all-reduce(f32[]{:T(128)} %get-tuple-element.3, f32[]{:T(128)} %get-tuple-element.2), channel_id=1, replica_groups=mesh['rows'=4,'cols'=64] {'cols'}, use_global_device_ids=true, to_apply=%region_2.3 | all-reduce | flops 2 | bytes 16 | tf_op jit(solution)/shard_map/psum | solution.py:27
  343.3 124.8 %psum.124 = f32[]{:T(128)} all-reduce(f32[]{:T(128)} %multiply_reduce_fusion.4), channel_id=1, replica_groups=mesh['rows'=4,'cols'=64] {'cols'}, use_global_device_ids=true, to_apply=%region_8.9 | all-reduce | flops 1 | bytes 8 | tf_op jit(solution)/shard_map/psum | solution.py:27
  469.5 0.9 fusion.39
  471.7 0.8 copy.31
  472.5 167.1 %all-reduce.9.cloned.1.call-done = f32[65536]{0:T(1024)} async-done(((f32[65536]{0:T(1024)}), f32[65536]{0:T(1024)}) %all-reduce.9.cloned.1.call-update) | async-done | bytes 262160 | tf_op jit(solution)/shard_map/psum | solution.py:85
  639.6 1.0 multiply_convert_fusion.2
  640.6 0.7 reshape.194
  641.4 1.1 fusion.24
  642.8 0.9 fusion.49
  643.8 0.7 convolution_bitcast_fusion.6
  644.5 8.4 psum.126
  653.5 125.2 %psum.127 = f32[]{:T(128)} all-reduce(f32[]{:T(128)} %multiply_reduce_fusion.3), channel_id=1, replica_groups=mesh['rows'=4,'cols'=64] {'cols'}, use_global_device_ids=true, to_apply=%region_12.13 | all-reduce | flops 1 | bytes 8 | tf_op jit(solution)/shard_map/psum | solution.py:88
  780.6 124.8 %psum.128 = f32[]{:T(128)} all-reduce(f32[]{:T(128)} %get-tuple-element.8), channel_id=1, replica_groups=mesh['rows'=4,'cols'=64] {'cols'}, use_global_device_ids=true, to_apply=%region_14.15 | all-reduce | flops 1 | bytes 8 | tf_op jit(solution)/shard_map/psum | solution.py:27
  906.8 0.9 fusion.36
  909.1 0.8 copy.33
  909.9 167.0 %all-reduce.11.cloned.1.call-done = f32[65536]{0:T(1024)} async-done(((f32[65536]{0:T(1024)}), f32[65536]{0:T(1024)}) %all-reduce.11.cloned.1.call-update) | async-done | bytes 262160 | tf_op jit(solution)/shard_map/psum | solution.py:85
  1076.9 1.0 multiply_convert_fusion.1
  1077.9 0.7 reshape.198
  1078.7 1.1 fusion.25
  1080.5 0.7 convolution_bitcast_fusion.5
  1081.2 8.4 psum.130
  1089.6 0.7 multiply_reduce_fusion.1
  1090.3 125.1 %psum.131 = f32[]{:T(128)} all-reduce(f32[]{:T(128)} %multiply_reduce_fusion.1), channel_id=1, replica_groups=mesh['rows'=4,'cols'=64] {'cols'}, use_global_device_ids=true, to_apply=%region_18.19 | all-reduce | flops 1 | bytes 8 | tf_op jit(solution)/shard_map/psum | solution.py:88
  1217.4 124.6 %psum.132 = f32[]{:T(128)} all-reduce(f32[]{:T(128)} %multiply_reduce_fusion), channel_id=1, replica_groups=mesh['rows'=4,'cols'=64] {'cols'}, use_global_device_ids=true, to_apply=%region_20.21 | all-reduce | flops 1 | bytes 8 | tf_op jit(solution)/shard_map/psum | solution.py:27
  1343.4 0.9 fusion.33
  1345.7 0.8 copy.35
  1346.5 167.2 %all-reduce.13.cloned.1.call-done = f32[65536]{0:T(1024)} async-done(((f32[65536]{0:T(1024)}), f32[65536]{0:T(1024)}) %all-reduce.13.cloned.1.call-update) | async-done | bytes 262160 | tf_op jit(solution)/shard_map/psum | solution.py:85
  1513.6 1.0 multiply_convert_fusion
  1514.7 0.8 fusion.26
  1515.9 0.9 fusion.45
  1516.9 0.7 convolution_bitcast_fusion.4
  1517.6 8.4 psum.134
  1526.0 1.4 fusion.72
  1527.4 125.2 %psum.135 = f32[]{:T(128)} all-reduce(f32[]{:T(128)} %fusion.72), channel_id=1, replica_groups=mesh['rows'=4,'cols'=64] {'cols'}, use_global_device_ids=true, to_apply=%region_24.25 | all-reduce | flops 1 | bytes 8 | tf_op jit(solution)/shard_map/psum | solution.py:88
  1653.9 1.4 dynamic-slice_subtract_fusion
  (92 shorter events, 11.8 us)
Async XLA Ops:
  7.2 2.6 copy-start
  7.2 2.9 copy-start.14
  7.2 2.9 copy-start.10
  7.2 195.1 %all-reduce.7.cloned.1.call-start = ((), (), s32[]{:S(2)}) async-start(), calls=%async_computation | async-start | bytes 524288 | tf_op jit(solution)/shard_map/psum | solution.py:85
  9.7 11.3 copy-start.2
  9.7 11.3 copy-start.6
  10.8 12.1 copy-start.7
  21.0 181.3 %copy-start.1 = (f32[65536]{0:T(1024)S(1)}, f32[65536]{0:T(1024)}, u32[]{:S(2)}) copy-start(f32[65536]{0:T(1024)} %param.13) | copy-start | bytes 786436
  24.0 615.6 %all-reduce.9.cloned.1.call-start = ((), (), s32[]{:S(2)}) async-start(), calls=%async_computation.1 | async-start | bytes 524288 | tf_op jit(solution)/shard_map/psum | solution.py:85
  205.1 265.3 %copy-start.11 = (s32[1,4]{1,0:T(1,128)S(1)}, s32[1,4]{1,0:T(1,128)}, u32[]{:S(2)}) copy-start(s32[1,4]{1,0:T(1,128)} %param.11) | copy-start | bytes 52
  205.1 265.3 %copy-start.15 = (s32[1,4]{1,0:T(1,128)S(1)}, s32[1,4]{1,0:T(1,128)}, u32[]{:S(2)}) copy-start(s32[1,4]{1,0:T(1,128)} %param.10) | copy-start | bytes 52
  472.5 604.5 %all-reduce.11.cloned.1.call-start = ((), (), s32[]{:S(2)}) async-start(), calls=%async_computation.2 | async-start | bytes 524288 | tf_op jit(solution)/shard_map/psum | solution.py:85
  642.4 265.3 %copy-start.12 = (s32[1,4]{1,0:T(1,128)S(1)}, s32[1,4]{1,0:T(1,128)}, u32[]{:S(2)}) copy-start(s32[1,4]{1,0:T(1,128)} %param.11) | copy-start | bytes 52
  642.5 265.3 %copy-start.16 = (s32[1,4]{1,0:T(1,128)S(1)}, s32[1,4]{1,0:T(1,128)}, u32[]{:S(2)}) copy-start(s32[1,4]{1,0:T(1,128)} %param.10) | copy-start | bytes 52
  643.8 264.9 %copy-start.8 = (s32[1,4]{1,0:T(1,128)S(1)}, s32[1,4]{1,0:T(1,128)}, u32[]{:S(2)}) copy-start(s32[1,4]{1,0:T(1,128)} %param.9) | copy-start | bytes 52
  780.6 129.2 %copy-start.3 = (f32[1024]{0:T(1024)}, f32[1024]{0:T(1024)S(1)}, u32[]{:S(2)}) copy-start(f32[1024]{0:T(1024)S(1)} %get-tuple-element.9) | copy-start | bytes 12292
  909.9 603.8 %all-reduce.13.cloned.1.call-start = ((), (), s32[]{:S(2)}) async-start(), calls=%async_computation.3 | async-start | bytes 524288 | tf_op jit(solution)/shard_map/psum | solution.py:85
  1078.7 1.5 copy-start.13
  1078.7 1.5 copy-start.17
  1078.7 138.1 %copy-start.4 = (f32[1024]{0:T(1024)S(1)}, f32[1024]{0:T(1024)}, u32[]{:S(2)}) copy-start(f32[1024]{0:T(1024)} %copy-done.3) | copy-start | bytes 12292
  1080.5 264.8 %copy-start.9 = (s32[1,4]{1,0:T(1,128)S(1)}, s32[1,4]{1,0:T(1,128)}, u32[]{:S(2)}) copy-start(s32[1,4]{1,0:T(1,128)} %param.9) | copy-start | bytes 52
  1089.6 256.9 %copy-start.5 = (f32[1024]{0:T(1024)}, f32[1024]{0:T(1024)S(1)}, u32[]{:S(2)}) copy-start(f32[1024]{0:T(1024)S(1)} %psum.130) | copy-start | bytes 12292
Sparse Core Ops, SparseCore 0:
  24.2 178.0 all-reduce.6
  472.6 166.9 all-reduce.8
  910.0 166.9 all-reduce.10
  1346.6 167.0 all-reduce.12
where the time goes:
time: 1660 us
  blocking collectives  918 us (55%)
  waiting for transfers between devices  680 us (41%)
  between operations  23.4 us (1%)
  matrix products  22.4 us (1%)
    psum x4, waiting for transfers between devices, per_device(): image_data = lax.psum(partial_data, 'cols')  679 us
    psum x4, blocking collectives, squared_norm(): return lax.psum(jnp.sum(values * values), 'cols')  499 us
    psum x3, blocking collectives, per_device(): curvature_sum = lax.psum(jnp.sum(direction * image_cells), 'cols')  376 us
    psum x5, blocking collectives, adjoint_part(): return lax.psum(cell_part, 'rows')  43.3 us
  transfers between devices with their start and end apart: 4, of which 4 were waited for; matrix products, arithmetic and copies ran while one was open for 0% of the time, Pallas kernels for 0%

commit v1 on v0

--- a/solution.py
+++ b/solution.py
@@ -82,7 +82,8 @@
             pick_rows.T.astype(jnp.float32), forward_products, precision=lax.Precision.HIGHEST
         )
         partial_data = summed.reshape(-1)
-        image_data = lax.psum(partial_data, "cols")
+        pieces = lax.all_gather(partial_data, "cols")
+        image_data = jnp.sum(pieces, axis=0)
         weighted = (squared * image_data).astype(jnp.bfloat16)
         image_cells = depth_weight * adjoint_part(weighted) + damping * direction
         curvature_sum = lax.psum(jnp.sum(direction * image_cells), "cols")

time: 1660 us -> 1420 us (0.86)
  waiting for transfers between devices: 680 us -> 378 us
  other arithmetic: 12.1 us -> 59.3 us
    psum x4 -> x0, waiting for transfers between devices: 679 us -> none  [per_device(): image_data = lax.psum(partial_data, 'cols')]
    all_gather x0 -> x4, waiting for transfers between devices: none -> 378 us  [per_device(): pieces = lax.all_gather(partial_data, 'cols')]
    reduce_sum x0 -> x4, other arithmetic: none -> 48 us  [per_device(): image_data = jnp.sum(pieces, axis=0)]
where the time goes in v1:
time: 1420 us
  blocking collectives  922 us (65%)
  waiting for transfers between devices  378 us (27%)
  other arithmetic  59.3 us (4%)
  matrix products  23.8 us (2%)
  between operations  22.7 us (2%)
    psum x4, blocking collectives, squared_norm(): return lax.psum(jnp.sum(values * values), 'cols')  500 us
    psum x3, blocking collectives, per_device(): curvature_sum = lax.psum(jnp.sum(direction * image_cells), 'cols')  379 us
    all_gather x4, waiting for transfers between devices, per_device(): pieces = lax.all_gather(partial_data, 'cols')  378 us
    reduce_sum x4, other arithmetic, per_device(): image_data = jnp.sum(pieces, axis=0)  48 us
    psum x5, blocking collectives, adjoint_part(): return lax.psum(cell_part, 'rows')  43.3 us
  transfers between devices with their start and end apart: 4, of which 4 were waited for; matrix products, arithmetic and copies ran while one was open for 0% of the time, Pallas kernels for 0%

profile of v1, /device:TPU:1, one launch (start us, length us, event | category | flops | bytes accessed | tf_op | source)
XLA Modules:
  0.0 1416.2 jit_solution(4283489816546856888)
XLA Ops:
  7.3 1.2 multiply_convert_fusion.4
  8.9 0.8 fusion.22
  11.4 9.5 psum.91
  21.0 0.9 fusion.42
  23.2 1.0 reshape.188
  24.3 102.8 %all-gather.9.cloned.1.call-done = f32[64,1,65536]{2,1,0:T(1,128)} async-done(((f32[1,1,65536]{2,1,0:T(1,128)}), f32[64,1,65536]{2,1,0:T(1,128)}) %all-gather.9.cloned.1.call-update) | async-done | bytes 16777232 | tf_op jit(solution)/shard_map/all_gather | solution.py:85
  127.2 12.0 reduce_sum.109
  139.2 1.0 multiply_convert_fusion.3
  140.1 0.7 reshape.177
  140.9 1.1 fusion.23
  142.3 0.9 fusion.54
  144.0 8.4 psum.93
  153.0 126.3 %all-reduce.1 = (f32[]{:T(128)}, f32[]{:T(128)}) all-reduce(f32[]{:T(128)} %get-tuple-element.3, f32[]{:T(128)} %get-tuple-element.2), channel_id=1, replica_groups=mesh['rows'=4,'cols'=64] {'cols'}, use_global_device_ids=true, to_apply=%region_2.3 | all-reduce | flops 2 | bytes 16 | tf_op jit(solution)/shard_map/psum | solution.py:27
  281.2 124.7 %psum.95 = f32[]{:T(128)} all-reduce(f32[]{:T(128)} %multiply_reduce_fusion.4), channel_id=1, replica_groups=mesh['rows'=4,'cols'=64] {'cols'}, use_global_device_ids=true, to_apply=%region_8.9 | all-reduce | flops 1 | bytes 8 | tf_op jit(solution)/shard_map/psum | solution.py:27
  407.2 0.9 fusion.39
  409.0 1.1 fusion.52
  410.1 2.0 reshape.190
  412.1 91.7 %all-gather.11.cloned.1.call-done = f32[64,1,65536]{2,1,0:T(1,128)} async-done(((f32[1,1,65536]{2,1,0:T(1,128)}), f32[64,1,65536]{2,1,0:T(1,128)}) %all-gather.11.cloned.1.call-update) | async-done | bytes 16777232 | tf_op jit(solution)/shard_map/all_gather | solution.py:85
  503.8 12.0 reduce_sum.112
  515.8 1.0 multiply_convert_fusion.2
  516.8 0.7 reshape.180
  517.5 1.1 fusion.24
  519.0 0.9 fusion.51
  520.6 8.4 psum.96
  529.7 126.3 %psum.97 = f32[]{:T(128)} all-reduce(f32[]{:T(128)} %multiply_reduce_fusion.3), channel_id=1, replica_groups=mesh['rows'=4,'cols'=64] {'cols'}, use_global_device_ids=true, to_apply=%region_12.13 | all-reduce | flops 1 | bytes 8 | tf_op jit(solution)/shard_map/psum | solution.py:89
  657.8 124.6 %psum.98 = f32[]{:T(128)} all-reduce(f32[]{:T(128)} %get-tuple-element.8), channel_id=1, replica_groups=mesh['rows'=4,'cols'=64] {'cols'}, use_global_device_ids=true, to_apply=%region_14.15 | all-reduce | flops 1 | bytes 8 | tf_op jit(solution)/shard_map/psum | solution.py:27
  783.7 0.9 fusion.36
  785.5 1.1 fusion.49
  786.6 2.0 reshape.192
  788.6 91.7 %all-gather.13.cloned.1.call-done = f32[64,1,65536]{2,1,0:T(1,128)} async-done(((f32[1,1,65536]{2,1,0:T(1,128)}), f32[64,1,65536]{2,1,0:T(1,128)}) %all-gather.13.cloned.1.call-update) | async-done | bytes 16777232 | tf_op jit(solution)/shard_map/all_gather | solution.py:85
  880.3 12.0 reduce_sum.115
  892.3 1.0 multiply_convert_fusion.1
  893.3 0.7 reshape.183
  894.0 1.1 fusion.25
  896.5 8.4 psum.99
  905.0 0.7 multiply_reduce_fusion.1
  905.6 126.2 %psum.100 = f32[]{:T(128)} all-reduce(f32[]{:T(128)} %multiply_reduce_fusion.1), channel_id=1, replica_groups=mesh['rows'=4,'cols'=64] {'cols'}, use_global_device_ids=true, to_apply=%region_18.19 | all-reduce | flops 1 | bytes 8 | tf_op jit(solution)/shard_map/psum | solution.py:89
  1033.8 124.7 %psum.101 = f32[]{:T(128)} all-reduce(f32[]{:T(128)} %multiply_reduce_fusion), channel_id=1, replica_groups=mesh['rows'=4,'cols'=64] {'cols'}, use_global_device_ids=true, to_apply=%region_20.21 | all-reduce | flops 1 | bytes 8 | tf_op jit(solution)/shard_map/psum | solution.py:27
  1159.7 0.9 fusion.33
  1161.5 1.1 fusion.46
  1162.6 2.0 reshape.194
  1164.6 91.8 %all-gather.15.cloned.1.call-done = f32[64,1,65536]{2,1,0:T(1,128)} async-done(((f32[1,1,65536]{2,1,0:T(1,128)}), f32[64,1,65536]{2,1,0:T(1,128)}) %all-gather.15.cloned.1.call-update) | async-done | bytes 16777232 | tf_op jit(solution)/shard_map/all_gather | solution.py:85
  1256.3 12.0 reduce_sum.118
  1268.4 1.0 multiply_convert_fusion
  1269.5 0.8 fusion.26
  1271.7 8.4 psum.102
  1280.7 126.3 %psum.103 = f32[]{:T(128)} all-reduce(f32[]{:T(128)} %fusion.76), channel_id=1, replica_groups=mesh['rows'=4,'cols'=64] {'cols'}, use_global_device_ids=true, to_apply=%region_24.25 | all-reduce | flops 1 | bytes 8 | tf_op jit(solution)/shard_map/psum | solution.py:89
  1408.3 1.4 dynamic-slice_subtract_fusion
  (106 shorter events, 14.8 us)
Async XLA Ops:
  7.2 2.6 copy-start
  7.2 2.9 copy-start.18
  7.2 2.9 copy-start.13
  7.2 120.0 %all-gather.9.cloned.1.call-start = ((), (), s32[]{:S(2)}) async-start(), calls=%async_computation | async-start | bytes 17039360 | tf_op jit(solution)/shard_map/all_gather | solution.py:85
  9.7 11.3 copy-start.2
  9.7 11.3 copy-start.8
  10.8 12.1 copy-start.10
  24.2 114.9 %copy-start.1 = (f32[65536]{0:T(1024)S(1)}, f32[65536]{0:T(1024)}, u32[]{:S(2)}) copy-start(f32[65536]{0:T(1024)} %param.13) | copy-start | bytes 786436
  24.3 479.6 %all-gather.11.cloned.1.call-start = ((), (), s32[]{:S(2)}) async-start(), calls=%async_computation.1 | async-start | bytes 17039360 | tf_op jit(solution)/shard_map/all_gather | solution.py:85
  142.0 266.2 %copy-start.14 = (s32[1,4]{1,0:T(1,128)S(1)}, s32[1,4]{1,0:T(1,128)}, u32[]{:S(2)}) copy-start(s32[1,4]{1,0:T(1,128)} %param.11) | copy-start | bytes 52
  142.0 266.2 %copy-start.19 = (s32[1,4]{1,0:T(1,128)S(1)}, s32[1,4]{1,0:T(1,128)}, u32[]{:S(2)}) copy-start(s32[1,4]{1,0:T(1,128)} %param.10) | copy-start | bytes 52
  412.1 468.3 %all-gather.13.cloned.1.call-start = ((), (), s32[]{:S(2)}) async-start(), calls=%async_computation.2 | async-start | bytes 17039360 | tf_op jit(solution)/shard_map/all_gather | solution.py:85
  518.6 266.0 %copy-start.15 = (s32[1,4]{1,0:T(1,128)S(1)}, s32[1,4]{1,0:T(1,128)}, u32[]{:S(2)}) copy-start(s32[1,4]{1,0:T(1,128)} %param.11) | copy-start | bytes 52
  518.6 266.0 %copy-start.20 = (s32[1,4]{1,0:T(1,128)S(1)}, s32[1,4]{1,0:T(1,128)}, u32[]{:S(2)}) copy-start(s32[1,4]{1,0:T(1,128)} %param.10) | copy-start | bytes 52
  520.0 265.5 %copy-start.11 = (s32[1,4]{1,0:T(1,128)S(1)}, s32[1,4]{1,0:T(1,128)}, u32[]{:S(2)}) copy-start(s32[1,4]{1,0:T(1,128)} %param.9) | copy-start | bytes 52
  657.8 130.7 %copy-start.3 = (f32[1024]{0:T(1024)}, f32[1024]{0:T(1024)S(1)}, u32[]{:S(2)}) copy-start(f32[1024]{0:T(1024)S(1)} %get-tuple-element.9) | copy-start | bytes 12292
  788.6 467.8 %all-gather.15.cloned.1.call-start = ((), (), s32[]{:S(2)}) async-start(), calls=%async_computation.3 | async-start | bytes 17039360 | tf_op jit(solution)/shard_map/all_gather | solution.py:85
  894.0 1.5 copy-start.16
  894.0 1.5 copy-start.21
  894.0 139.1 %copy-start.4 = (f32[1024]{0:T(1024)S(1)}, f32[1024]{0:T(1024)}, u32[]{:S(2)}) copy-start(f32[1024]{0:T(1024)} %copy-done.3) | copy-start | bytes 12292
  895.8 265.6 %copy-start.12 = (s32[1,4]{1,0:T(1,128)S(1)}, s32[1,4]{1,0:T(1,128)}, u32[]{:S(2)}) copy-start(s32[1,4]{1,0:T(1,128)} %param.9) | copy-start | bytes 52
  905.0 259.6 %copy-start.6 = (f32[1024]{0:T(1024)}, f32[1024]{0:T(1024)S(1)}, u32[]{:S(2)}) copy-start(f32[1024]{0:T(1024)S(1)} %psum.99) | copy-start | bytes 12292
  1269.3 1.4 copy-start.17
  1269.4 1.4 copy-start.22
  1269.4 10.7 copy-start.5
  1269.4 10.7 copy-start.7
  1269.4 138.9 %copy-start.9 = (f32[1024]{0:T(1024)S(1)}, f32[1024]{0:T(1024)}, u32[]{:S(2)}) copy-start(f32[1024]{0:T(1024)} %param.15) | copy-start | bytes 12292
Sparse Core Ops, SparseCore 0:
  24.4 102.7 all-gather.8
  412.2 91.6 all-gather.10
  788.7 91.6 all-gather.12
  1164.7 91.6 all-gather.14
